TPU v7x, 32 devices: a whole 2x2x4 slice. The times are simulated.
32 devices in a mesh: groups: 2 (over y), space: 8 (over z, x), heads: 2 (over core).
Axes of the slice: x: 2, y: 2, z: 4, core: 2. Of those that a mesh axis runs over, the one named last changes fastest.
Arguments:
- queries: bfloat16 [2400, 1536], P(('groups', 'space'), 'heads'), parts along dimension 0, may hold values from -16 to 16
- latent_keys: bfloat16 [2400, 1536], P(('groups', 'space'), 'heads'), parts along dimension 0, may hold values from -9 to 9
- latent_values: bfloat16 [2400, 1536], P(('groups', 'space'), 'heads'), parts along dimension 0, may hold values from -6 to 6
- prompt: bfloat16 [512, 3072], P('groups'), parts along dimension 0, may hold values from -44 to 44
- key_weight: bfloat16 [3072, 1536], P('space', 'heads'), may hold values from -0.15625 to 0.15625
- value_weight: bfloat16 [3072, 1536], P('space', 'heads'), may hold values from -0.15625 to 0.15625
- out_weight: bfloat16 [1536, 3072], P('heads', 'space'), may hold values from -0.21875 to 0.21875
- tile_owner: int32 [16], P('groups'), parts along dimension 0, may hold values from 0 to 7, as said below
Outputs:
- block_output: bfloat16 [2400, 3072], P(('groups', 'space'), 'heads'), parts along dimension 0
There are 2 independent parts, one for each index of `groups`. A program takes and returns all parts, laid end to end along the dimension named above; an argument that names none is the same for every part. Nothing has to cross between parts.
Inputs may be any that keep to these rules, and one draw needn't show every extreme that they name: `tile_owner`: tile t = i * 2 + j of the 4 x 2 grid is held by slot a * 2 + b, with a = (i + r) mod 4 or a = (3 - i + r) mod 4 for one r, and b = j or b = 1 - j; r and each of the two alternatives are the same for all tiles.
All inputs are finite; a program needn't handle non-finite values.
Results may differ from a plain program's by a relative error of at most 0.0081.
Values may be sent and summed in bfloat16 or wider, within the bound.
A program may use at most 64 MiB of HBM per device.

v0:
```python
import jax
import jax.numpy as jnp
from jax import lax
from jax.sharding import PartitionSpec as P

HD = 128
RT = 16
RH = 56
TILE = 5
rope_theta = 256.0
eps_norm = 1e-06
masked_score = -1e30


def shifted(value, axis, steps):
    count = lax.axis_size(axis)
    pairs = [(source, (source + steps) % count) for source in range(count)]
    return lax.ppermute(value, axis, pairs)


def rope_tables(frame_pos, height_pos, width_pos):
    pairs_time = jnp.arange(RT // 2, dtype=jnp.float32)
    pairs_space = jnp.arange(RH // 2, dtype=jnp.float32)
    freq_time = rope_theta ** (-2.0 * pairs_time / RT)
    freq_space = rope_theta ** (-2.0 * pairs_space / RH)
    angles = jnp.concatenate(
        [
            frame_pos[:, None] * freq_time[None, :],
            height_pos[:, None] * freq_space[None, :],
            width_pos[:, None] * freq_space[None, :],
        ],
        axis=1,
    )
    return (jnp.cos(angles), jnp.sin(angles))


def rotate(stacked, cosine, sine_table):
    row_count = stacked.shape[0]
    head_total = stacked.shape[1]
    paired = stacked.reshape(row_count, head_total, HD // 2, 2)
    even_part = paired[..., 0]
    odd_part = paired[..., 1]
    cos_rows = cosine[:, None, :]
    sin_rows = sine_table[:, None, :]
    turned = jnp.stack(
        [even_part * cos_rows - odd_part * sin_rows, even_part * sin_rows + odd_part * cos_rows],
        axis=-1,
    )
    return turned.reshape(row_count, head_total * HD)


def normalize_keys(summed, head_total):
    row_count = summed.shape[0]
    half_width = summed.shape[1] // 2
    key_part = summed[:, :half_width].reshape(row_count, head_total, HD)
    key_part = key_part * lax.rsqrt(
        jnp.mean(key_part * key_part, axis=-1, keepdims=True) + eps_norm
    )
    return jnp.concatenate(
        [key_part.reshape(row_count, half_width), summed[:, half_width:]], axis=1
    ).astype(jnp.bfloat16)


def body(
    queries, latent_keys, latent_values, prompt, key_weight, value_weight, out_weight, tile_owner
):
    spaces = lax.axis_size("space")
    device = lax.axis_index("space")
    grid_h = min(8, spaces // 2)
    grid_w = spaces // grid_h
    tok_rows = queries.shape[0]
    head_width = queries.shape[1]
    head_count = head_width // HD
    tile_total = tile_owner.shape[0]
    tile_index = jnp.arange(tile_total, dtype=jnp.int32)
    own_tile = jnp.sum(jnp.where(tile_owner == device, tile_index, 0))
    tile_row = own_tile // grid_w
    tile_col = own_tile % grid_w
    anchor_slot = tile_owner[0]
    right_slot = tile_owner[min(1, tile_total - 1)]
    lower_slot = tile_owner[min(grid_w, tile_total - 1)]
    col_sign = jnp.where(right_slot % grid_w - anchor_slot % grid_w == -1, -1, 1)
    row_sign = jnp.where((lower_slot // grid_w - anchor_slot // grid_w) % grid_h == 1, 1, -1)
    cell_index = jnp.arange(tok_rows, dtype=jnp.int32)
    frame_pos = (cell_index // (TILE * TILE)).astype(jnp.float32)
    height_pos = (tile_row * TILE + cell_index // TILE % TILE).astype(jnp.float32)
    width_pos = (tile_col * TILE + cell_index % TILE).astype(jnp.float32)
    cosine, sine_table = rope_tables(frame_pos, height_pos, width_pos)
    query_rot = rotate(
        queries.astype(jnp.float32).reshape(tok_rows, head_count, HD), cosine, sine_table
    ).astype(jnp.bfloat16)
    key_rot = rotate(
        latent_keys.astype(jnp.float32).reshape(tok_rows, head_count, HD), cosine, sine_table
    ).astype(jnp.bfloat16)
    width_rows = key_weight.shape[0]
    text_cols = lax.dynamic_slice_in_dim(prompt, device * width_rows, width_rows, 1)
    both_weights = jnp.concatenate([key_weight, value_weight], axis=1)
    partial_text = jnp.dot(text_cols, both_weights, preferred_element_type=jnp.float32)
    summed_text = lax.psum(partial_text, "space")
    text_kv = normalize_keys(summed_text, head_count)
    kv_own = jnp.concatenate([key_rot, latent_values], axis=1)
    blocks = []
    valid_parts = []
    for row_step in (-1, 0, 1):
        for col_step in (-1, 0, 1):
            if row_step == 0 and col_step == 0:
                fetched = kv_own
            else:
                fetched = shifted(kv_own, "space", -(row_step * grid_w + col_step))
            near_row = tile_row + row_sign * row_step
            near_col = tile_col + col_sign * col_step
            inside = (near_row >= 0) & (near_row < grid_h) & (near_col >= 0) & (near_col < grid_w)
            blocks.append(fetched)
            valid_parts.append(jnp.zeros((tok_rows,), jnp.int32) + inside.astype(jnp.int32))
    blocks.append(text_kv)
    valid_parts.append(jnp.ones((text_kv.shape[0],), jnp.int32))
    keys_all = jnp.concatenate(blocks, axis=0)
    key_valid = jnp.concatenate(valid_parts, axis=0)
    score_scale = HD ** (-0.5)
    head_outputs = []
    for head_index in range(head_count):
        head_start = head_index * HD
        query_slice = query_rot[:, head_start : head_start + HD]
        key_slice = keys_all[:, head_start : head_start + HD]
        value_slice = keys_all[:, head_width + head_start : head_width + head_start + HD]
        scores = (
            lax.dot_general(
                query_slice, key_slice, (((1,), (1,)), ((), ())), preferred_element_type=jnp.float32
            )
            * score_scale
        )
        scores = jnp.where(key_valid[None, :] > 0, scores, masked_score)
        top_score = jnp.max(scores, axis=-1, keepdims=True)
        exponent = jnp.exp(scores - top_score)
        weights = (exponent / jnp.sum(exponent, axis=-1, keepdims=True)).astype(jnp.bfloat16)
        head_outputs.append(
            jnp.dot(weights, value_slice, preferred_element_type=jnp.float32).astype(jnp.bfloat16)
        )
    attended = jnp.concatenate(head_outputs, axis=1)
    partial_out = jnp.dot(
        attended,
        lax.all_gather(out_weight, "space", axis=1, tiled=True),
        preferred_element_type=jnp.float32,
    )
    summed_out = lax.psum_scatter(
        partial_out.astype(jnp.bfloat16), "heads", scatter_dimension=1, tiled=True
    )
    return summed_out


def solution(mesh):
    in_specs = (
        P(("groups", "space"), "heads"),
        P(("groups", "space"), "heads"),
        P(("groups", "space"), "heads"),
        P("groups", None),
        P("space", "heads"),
        P("space", "heads"),
        P("heads", "space"),
        P("groups"),
    )
    out_specs = P(("groups", "space"), "heads")
    return jax.shard_map(body, mesh=mesh, in_specs=in_specs, out_specs=out_specs, check_vma=False)
```

profile of v0, /device:TPU:0, one launch (start us, length us, event | category | flops | bytes accessed | tf_op | source)
XLA Modules:
  0.0 252.2 jit_solution(18399292161967376809)
XLA Ops:
  6.6 1.4 copy-done
  7.9 3.0 %fusion.6 = f32[256,1536]{1,0:T(8,128)} fusion(bf16[384,768]{1,0:T(8,128)(2,1)} %param.13, bf16[384,768]{1,0:T(8,128)(2,1)} %param.12, bf16[256,3072]{1,0:T(8,128)(2,1)S(1)} %copy-done, s32[]{:T(128)S(6)} %select_n.110), kind=kOutput, calls=%fused_computation.13 | convolution fusion | flops 304349184 | bytes 2949124 | tf_op jit(solution)/shard_map/dot_general | solution.py:98
  11.0 0.7 all-gather.2.cloned.1.call-update
  11.7 0.6 fusion.51
  15.7 2.0 copy.10
  17.7 1.6 reshape.202
  19.7 2.7 %subtract_convert_fusion.1 = (bf16[150,6,64,1]{0,3,2,1:T(2,128)(2,1)S(1)}, bf16[150,6,64,1]{0,3,2,1:T(2,128)(2,1)}, bf16[150,6,64,1]{0,3,2,1:T(2,128)(2,1)S(1)}, bf16[150,6,64,1]{0,3,2,1:T(2,128)(2,1)S(1)}) fusion(f32[150,6,64,2]{0,3,2,1:T(2,128)S(1)} %reshape.201, f32[150,64]{0,1:T(8,128)S(1)} %get-tuple-element.12, f32[150,64]{0,1:T(8,128)S(1)} %get-tuple-element.11, ...), kind=kLoop, calls=%fused_computation.69 | loop fusion | flops 921600 | bytes 1459200 | tf_op jit(solution)/shard_map/convert.7
  22.5 1.0 pad_maximum_fusion.3
  24.0 1.7 pad_maximum_fusion.1
  25.7 4.0 %collective-permute-start = (bf16[150,1536]{1,0:T(8,128)(2,1)}, bf16[150,1536]{1,0:T(8,128)(2,1)}, u32[]{:S(2)}, u32[]{:S(2)}) collective-permute-start(bf16[150,1536]{1,0:T(8,128)(2,1)} %pad_maximum_fusion.1), channel_id=1, source_target_pairs={{0,6},{2,8},{4,10},{6,12},{8,14},{10,0},{12,2},{14,4},{1,7},{3,9},... | collective-permute-start | bytes 1382408 | tf_op jit(solution)/shard_map/ppermute | solution.py:18
  29.7 1.6 collective-permute-start.1
  31.3 1.5 collective-permute-start.2
  32.8 3.2 %collective-permute-start.3 = (bf16[150,1536]{1,0:T(8,128)(2,1)}, bf16[150,1536]{1,0:T(8,128)(2,1)}, u32[]{:S(2)}, u32[]{:S(2)}) collective-permute-start(bf16[150,1536]{1,0:T(8,128)(2,1)} %pad_maximum_fusion.1), channel_id=1, source_target_pairs={{0,14},{2,0},{4,2},{6,4},{8,6},{10,8},{12,10},{14,12},{1,15},{3,1}... | collective-permute-start | bytes 1382408 | tf_op jit(solution)/shard_map/ppermute | solution.py:18
  36.5 0.6 fusion.54
  43.3 2.0 pad_maximum_fusion.2
  45.3 1.1 convert_element_type.110
  46.6 91.5 %all-reduce.2.cloned.1.call-done = f32[256,1536]{1,0:T(8,128)} async-done(((f32[256,1536]{1,0:T(8,128)}), f32[256,1536]{1,0:T(8,128)}) %all-reduce.2.cloned.1.call-update) | async-done | bytes 1572880 | tf_op jit(solution)/shard_map/psum | solution.py:99
  138.1 1.2 slice_multiply_fusion
  140.0 1.2 slice.180
  141.2 3.0 %collective-permute-start.5 = (bf16[150,1536]{1,0:T(8,128)(2,1)}, bf16[150,1536]{1,0:T(8,128)(2,1)S(1)}, u32[]{:S(2)}, u32[]{:S(2)}) collective-permute-start(bf16[150,1536]{1,0:T(8,128)(2,1)} %pad_maximum_fusion.1), channel_id=1, source_target_pairs={{0,10},{2,12},{4,14},{6,0},{8,2},{10,4},{12,6},{14,8},{1,11},{3,13... | collective-permute-start | bytes 1382408 | tf_op jit(solution)/shard_map/ppermute | solution.py:18
  144.1 1.2 multiply_convert_fusion
  145.4 16.0 %collective-permute-done.5 = bf16[150,1536]{1,0:T(8,128)(2,1)S(1)} collective-permute-done((bf16[150,1536]{1,0:T(8,128)(2,1)}, bf16[150,1536]{1,0:T(8,128)(2,1)S(1)}, u32[]{:S(2)}, u32[]{:S(2)}) %collective-permute-start.5) | collective-permute-done | bytes 460832 | tf_op jit(solution)/shard_map/ppermute | solution.py:18
  161.5 34.4 %concatenate.39 = bf16[1606,1536]{1,0:T(8,128)(2,1)} concatenate(bf16[150,1536]{1,0:T(8,128)(2,1)} %collective-permute-done, bf16[150,1536]{1,0:T(8,128)(2,1)} %collective-permute-done.1, bf16[150,1536]{1,0:T(8,128)(2,1)} %collective-permute-done.2, bf16[150,1536]{1,0:T(8,128)(2,1)} %collective-permute-done.2, bf16[150,1536]{1,0:T(8,128)(2,1)} %pad_maximum_fusion.1, ...), dimensions={0} | concatenate | bytes 9867264 | tf_op jit(solution)/shard_map/concatenate | solution.py:117
  195.9 1.6 fusion.55
  197.8 1.6 fusion.56
  199.7 1.7 fusion.57
  201.7 1.6 fusion.58
  203.5 1.6 fusion.59
  205.4 1.6 fusion.60
  209.9 22.8 %all-gather.2.cloned.1.call-done = bf16[768,3072]{1,0:T(8,128)(2,1)} async-done(((bf16[768,384]{1,0:T(8,128)(2,1)}), bf16[768,3072]{1,0:T(8,128)(2,1)}) %all-gather.2.cloned.1.call-update) | async-done | bytes 4718608 | tf_op jit(solution)/shard_map/all_gather | solution.py:142
  232.6 4.2 %convolution_convert_fusion = bf16[150,3072]{1,0:T(8,128)(2,1)} fusion(bf16[150,768]{1,0:T(8,128)(2,1)S(1)} %fusion.10, bf16[768,3072]{1,0:T(8,128)(2,1)} %all-gather.2.cloned.1.call-done), kind=kOutput, calls=%fused_computation | convolution fusion | flops 708249600 | bytes 5870592 | tf_op jit(solution)/shard_map/dot_general | solution.py:140
  236.8 8.8 %reduce-scatter.2.cloned.1.call-done = bf16[150,1536]{1,0:T(8,128)(2,1)} async-done(((bf16[150,3072]{1,0:T(8,128)(2,1)}), bf16[150,1536]{1,0:T(8,128)(2,1)}) %reduce-scatter.2.cloned.1.call-update) | async-done | bytes 460816 | tf_op jit(solution)/shard_map/reduce_scatter | solution.py:145
  (59 shorter events, 7.3 us)
Async XLA Ops:
  6.5 1.4 copy-start
  6.5 5.2 %copy-start.3 = (s32[8]{0:T(128)S(1)}, s32[8]{0:T(128)}, u32[]{:S(2)}) copy-start(s32[8]{0:T(128)} %param.15) | copy-start | bytes 100
  6.5 8.4 %copy-start.2 = (bf16[150,768]{1,0:T(8,128)(2,1)S(1)}, bf16[150,768]{1,0:T(8,128)(2,1)}, u32[]{:S(2)}) copy-start(bf16[150,768]{1,0:T(8,128)(2,1)} %param.8) | copy-start | bytes 691204
  6.5 131.5 %all-reduce.2.cloned.1.call-start = ((), (), s32[]{:S(2)}) async-start(), calls=%async_computation.1 | async-start | bytes 3145728 | tf_op jit(solution)/shard_map/psum | solution.py:99
  10.9 221.7 %all-gather.2.cloned.1.call-start = ((), (), s32[]{:S(2)}) async-start(), calls=%async_computation.2 | async-start | bytes 5308416 | tf_op jit(solution)/shard_map/all_gather | solution.py:142
  11.7 234.0 %reduce-scatter.2.cloned.1.call-start = ((), (), s32[]{:S(2)}) async-start(), calls=%async_computation.3 | async-start | bytes 1400832 | tf_op jit(solution)/shard_map/reduce_scatter | solution.py:145
  25.7 115.4 %collective-permute-start = (bf16[150,1536]{1,0:T(8,128)(2,1)}, bf16[150,1536]{1,0:T(8,128)(2,1)}, u32[]{:S(2)}, u32[]{:S(2)}) collective-permute-start(bf16[150,1536]{1,0:T(8,128)(2,1)} %pad_maximum_fusion.1), channel_id=1, source_target_pairs={{0,6},{2,8},{4,10},{6,12},{8,14},{10,0},{12,2},{14,4},{1,7},{3,9},... | collective-permute-start | bytes 1382408 | tf_op jit(solution)/shard_map/ppermute | solution.py:18
  29.7 115.7 %collective-permute-start.1 = (bf16[150,1536]{1,0:T(8,128)(2,1)}, bf16[150,1536]{1,0:T(8,128)(2,1)}, u32[]{:S(2)}, u32[]{:S(2)}) collective-permute-start(bf16[150,1536]{1,0:T(8,128)(2,1)} %pad_maximum_fusion.1), channel_id=1, source_target_pairs={{0,4},{2,6},{4,8},{6,10},{8,12},{10,14},{12,0},{14,2},{1,5},{3,7},... | collective-permute-start | bytes 1382408 | tf_op jit(solution)/shard_map/ppermute | solution.py:18
  31.3 114.1 %collective-permute-start.2 = (bf16[150,1536]{1,0:T(8,128)(2,1)}, bf16[150,1536]{1,0:T(8,128)(2,1)}, u32[]{:S(2)}, u32[]{:S(2)}) collective-permute-start(bf16[150,1536]{1,0:T(8,128)(2,1)} %pad_maximum_fusion.1), channel_id=1, source_target_pairs={{0,2},{2,4},{4,6},{6,8},{8,10},{10,12},{12,14},{14,0},{1,3},{3,5},... | collective-permute-start | bytes 1382408 | tf_op jit(solution)/shard_map/ppermute | solution.py:18
  32.8 112.6 %collective-permute-start.3 = (bf16[150,1536]{1,0:T(8,128)(2,1)}, bf16[150,1536]{1,0:T(8,128)(2,1)}, u32[]{:S(2)}, u32[]{:S(2)}) collective-permute-start(bf16[150,1536]{1,0:T(8,128)(2,1)} %pad_maximum_fusion.1), channel_id=1, source_target_pairs={{0,14},{2,0},{4,2},{6,4},{8,6},{10,8},{12,10},{14,12},{1,15},{3,1}... | collective-permute-start | bytes 1382408 | tf_op jit(solution)/shard_map/ppermute | solution.py:18
  36.0 109.4 %collective-permute-start.4 = (bf16[150,1536]{1,0:T(8,128)(2,1)}, bf16[150,1536]{1,0:T(8,128)(2,1)}, u32[]{:S(2)}, u32[]{:S(2)}) collective-permute-start(bf16[150,1536]{1,0:T(8,128)(2,1)} %pad_maximum_fusion.1), channel_id=1, source_target_pairs={{0,12},{2,14},{4,0},{6,2},{8,4},{10,6},{12,8},{14,10},{1,13},{3,15... | collective-permute-start | bytes 1382408 | tf_op jit(solution)/shard_map/ppermute | solution.py:18
  141.2 20.3 %collective-permute-start.5 = (bf16[150,1536]{1,0:T(8,128)(2,1)}, bf16[150,1536]{1,0:T(8,128)(2,1)S(1)}, u32[]{:S(2)}, u32[]{:S(2)}) collective-permute-start(bf16[150,1536]{1,0:T(8,128)(2,1)} %pad_maximum_fusion.1), channel_id=1, source_target_pairs={{0,10},{2,12},{4,14},{6,0},{8,2},{10,4},{12,6},{14,8},{1,11},{3,13... | collective-permute-start | bytes 1382408 | tf_op jit(solution)/shard_map/ppermute | solution.py:18
  199.6 7.7 %copy-start.1 = (bf16[1606,1536]{1,0:T(8,128)(2,1)S(1)}, bf16[1606,1536]{1,0:T(8,128)(2,1)}, u32[]{:S(2)}) copy-start(bf16[1606,1536]{1,0:T(8,128)(2,1)} %concatenate.39) | copy-start | bytes 14800900
Sparse Core Ops, SparseCore 0:
  11.1 126.9 all-reduce.1
  140.1 92.4 all-gather.1
  237.0 8.6 reduce-scatter.1
where the time goes:
time: 254 us; the launch traced here: 252 us
  waiting for transfers between devices  140 us (55%)
  local copies, waits for them, and re-layouts  44.1 us (17%)
  between operations  22.3 us (9%)
  matrix products  19.3 us (8%)
  starting transfers between devices  13.8 us (5%)
  other arithmetic  12.8 us (5%)
    psum x1, waiting for transfers between devices, body(): summed_text = lax.psum(partial_text, 'space')  91.5 us
    concatenate x1, local copies, waits for them, and re-layouts, body(): keys_all = jnp.concatenate(blocks, axis=0)  34.4 us
    all_gather x1, waiting for transfers between devices, body(): lax.all_gather(out_weight, 'space', axis=1, tiled=True)  22.8 us
    ppermute x6, waiting for transfers between devices, shifted(): return lax.ppermute(value, axis, pairs)  16.1 us
    ppermute x6, starting transfers between devices, shifted(): return lax.ppermute(value, axis, pairs)  13.7 us
    dot_general x6, matrix products, body(): lax.dot_general(query_slice, key_slice, (((1,), (1,)), ((), ())), preferr...  9.63 us
    reduce_scatter x1, waiting for transfers between devices, body(): lax.psum_scatter(partial_out.astype(jnp.bfloat16), 'heads', scatter_dimen...  8.8 us
  transfers between devices with their start and end apart: 9, of which 4 were waited for; matrix products, arithmetic and copies ran while one was open for 27% of the time, Pallas kernels for 0%

commit v1 on v0

--- a/solution.py
+++ b/solution.py
@@ -1,3 +1,4 @@
+import functools
 import jax
 import jax.numpy as jnp
 from jax import lax
@@ -10,6 +11,14 @@
 rope_theta = 256.0
 eps_norm = 1e-06
 masked_score = -1e30
+
+
+def get_widths_by_axis(frame_in, mesh_name):
+    tmp = jax.lax.all_gather(frame_in, axis_name=mesh_name)
+    return jnp.sum(tmp, axis=0)
+
+
+zone_check = functools.partial(get_widths_by_axis, mesh_name="space")
 
 
 def shifted(value, axis, steps):
@@ -96,7 +105,7 @@
     text_cols = lax.dynamic_slice_in_dim(prompt, device * width_rows, width_rows, 1)
     both_weights = jnp.concatenate([key_weight, value_weight], axis=1)
     partial_text = jnp.dot(text_cols, both_weights, preferred_element_type=jnp.float32)
-    summed_text = lax.psum(partial_text, "space")
+    summed_text = zone_check(partial_text)
     text_kv = normalize_keys(summed_text, head_count)
     kv_own = jnp.concatenate([key_rot, latent_values], axis=1)
     blocks = []

time: 254 us -> 361 us (1.42)
  waiting for transfers between devices: 140 us -> 236 us
  other arithmetic: 12.8 us -> 19.9 us
  local copies, waits for them, and re-layouts: 44.1 us -> 48.9 us
    all_gather x0 -> x1, waiting for transfers between devices: none -> 193 us  [get_widths_by_axis(): tmp = jax.lax.all_gather(frame_in, axis_name=mesh_name)]
    psum x1 -> x0, waiting for transfers between devices: 91.5 us -> none  [body(): summed_text = lax.psum(partial_text, 'space')]
    all_gather x1, waiting for transfers between devices: 22.8 us -> 7.3 us  [body(): lax.all_gather(out_weight, 'space', axis=1, tiled=True)]
    ppermute x6, waiting for transfers between devices: 16.1 us -> 23 us  [shifted(): return lax.ppermute(value, axis, pairs)]
    reduce_sum x0 -> x1, other arithmetic: none -> 6.17 us  [get_widths_by_axis(): return jnp.sum(tmp, axis=0)]
  transfers between devices with their start and end apart: 9 -> 9, of which waited for: 4 -> 4; matrix products, arithmetic and copies ran while one was open for 27% -> 22% of each run, Pallas kernels for 0% -> 0%
where the time goes in v1:
time: 361 us; the launch traced here: 359 us
  waiting for transfers between devices  236 us (65%)
  local copies, waits for them, and re-layouts  48.9 us (14%)
  between operations  22.9 us (6%)
  other arithmetic  19.9 us (6%)
  matrix products  19.4 us (5%)
  starting transfers between devices  12.4 us (3%)
    all_gather x1, waiting for transfers between devices, get_widths_by_axis(): tmp = jax.lax.all_gather(frame_in, axis_name=mesh_name)  193 us
    concatenate x1, local copies, waits for them, and re-layouts, body(): keys_all = jnp.concatenate(blocks, axis=0)  36.2 us
    ppermute x6, waiting for transfers between devices, shifted(): return lax.ppermute(value, axis, pairs)  23 us
    ppermute x6, starting transfers between devices, shifted(): return lax.ppermute(value, axis, pairs)  12.3 us
    reduce_scatter x1, waiting for transfers between devices, body(): lax.psum_scatter(partial_out.astype(jnp.bfloat16), 'heads', scatter_dimen...  11.9 us
    dot_general x6, matrix products, body(): lax.dot_general(query_slice, key_slice, (((1,), (1,)), ((), ())), preferr...  9.65 us
    all_gather x1, waiting for transfers between devices, body(): lax.all_gather(out_weight, 'space', axis=1, tiled=True)  7.3 us
  transfers between devices with their start and end apart: 9, of which 4 were waited for; matrix products, arithmetic and copies ran while one was open for 22% of the time, Pallas kernels for 0%

profile of v1, /device:TPU:0, one launch (start us, length us, event | category | flops | bytes accessed | tf_op | source)
XLA Modules:
  0.0 359.2 jit_solution(8512620936046549972)
XLA Ops:
  6.6 1.4 copy-done
  7.9 3.0 fusion.6
  15.7 1.1 copy.13
  16.8 1.6 reshape.202
  18.9 2.8 subtract_convert_fusion.1
  21.7 1.0 pad_maximum_fusion.3
  23.2 1.8 pad_maximum_fusion.1
  24.9 4.0 %collective-permute-start = (bf16[150,1536]{1,0:T(8,128)(2,1)}, bf16[150,1536]{1,0:T(8,128)(2,1)}, u32[]{:S(2)}, u32[]{:S(2)}) collective-permute-start(bf16[150,1536]{1,0:T(8,128)(2,1)} %pad_maximum_fusion.1), channel_id=1, source_target_pairs={{0,6},{2,8},{4,10},{6,12},{8,14},{10,0},{12,2},{14,4},{1,7},{3,9},... | collective-permute-start | bytes 1382408 | tf_op jit(solution)/shard_map/ppermute | solution.py:27
  28.9 1.6 collective-permute-start.1
  30.5 1.5 collective-permute-start.2
  32.1 3.2 collective-permute-start.3
  43.2 2.0 pad_maximum_fusion.2
  45.2 1.1 convert_element_type.110
  46.5 192.8 %all-gather.6.cloned.1.call-done = f32[2048,1536]{1,0:T(8,128)} async-done(((f32[256,1536]{1,0:T(8,128)}), f32[2048,1536]{1,0:T(8,128)}) %all-gather.6.cloned.1.call-update) | async-done | bytes 12582928 | tf_op jit(solution)/shard_map/all_gather | solution.py:17
  239.3 6.2 %reduce_sum.82 = f32[256,1536]{1,0:T(8,128)S(1)} reduce(f32[8,256,1536]{2,1,0:T(8,128)} %bitcast.16, f32[]{:T(128)} %constant.117.clone.1), dimensions={0}, to_apply=%region_1.2 | reduce | flops 2752512 | bytes 14155780 | tf_op jit(solution)/shard_map/reduce_sum | solution.py:18
  246.4 2.4 copy.15
  248.8 1.2 reduce_sum.83
  250.0 1.0 mul.191
  251.0 2.3 copy.16
  253.3 1.5 collective-permute-start.5
  254.8 1.2 multiply_convert_fusion
  256.1 23.0 %collective-permute-done.5 = bf16[150,1536]{1,0:T(8,128)(2,1)} collective-permute-done((bf16[150,1536]{1,0:T(8,128)(2,1)}, bf16[150,1536]{1,0:T(8,128)(2,1)}, u32[]{:S(2)}, u32[]{:S(2)}) %collective-permute-start.5) | collective-permute-done | bytes 460832 | tf_op jit(solution)/shard_map/ppermute | solution.py:27
  279.1 36.2 %concatenate.39 = bf16[1606,1536]{1,0:T(8,128)(2,1)} concatenate(bf16[150,1536]{1,0:T(8,128)(2,1)} %collective-permute-done, bf16[150,1536]{1,0:T(8,128)(2,1)} %collective-permute-done.1, bf16[150,1536]{1,0:T(8,128)(2,1)} %collective-permute-done.2, bf16[150,1536]{1,0:T(8,128)(2,1)} %collective-permute-done.2, bf16[150,1536]{1,0:T(8,128)(2,1)} %pad_maximum_fusion.1, ...), dimensions={0} | concatenate | bytes 9867264 | tf_op jit(solution)/shard_map/concatenate | solution.py:126
  315.3 1.7 fusion.55
  317.3 1.6 fusion.56
  319.2 1.6 fusion.57
  321.0 1.6 fusion.58
  322.9 1.6 fusion.59
  324.8 1.6 fusion.60
  329.3 7.3 %all-gather.4.cloned.1.call-done = bf16[768,3072]{1,0:T(8,128)(2,1)} async-done(((bf16[768,384]{1,0:T(8,128)(2,1)}), bf16[768,3072]{1,0:T(8,128)(2,1)}) %all-gather.4.cloned.1.call-update) | async-done | bytes 4718608 | tf_op jit(solution)/shard_map/all_gather | solution.py:151
  336.6 4.2 %convolution_convert_fusion = bf16[150,3072]{1,0:T(8,128)(2,1)} fusion(bf16[150,768]{1,0:T(8,128)(2,1)S(1)} %fusion.10, bf16[768,3072]{1,0:T(8,128)(2,1)} %all-gather.4.cloned.1.call-done), kind=kOutput, calls=%fused_computation | convolution fusion | flops 708249600 | bytes 5870592 | tf_op jit(solution)/shard_map/dot_general | solution.py:149
  340.8 11.9 %reduce-scatter.2.cloned.1.call-done = bf16[150,1536]{1,0:T(8,128)(2,1)} async-done(((bf16[150,3072]{1,0:T(8,128)(2,1)}), bf16[150,1536]{1,0:T(8,128)(2,1)}) %reduce-scatter.2.cloned.1.call-update) | async-done | bytes 460816 | tf_op jit(solution)/shard_map/reduce_scatter | solution.py:154
  (65 shorter events, 9.7 us)
Async XLA Ops:
  6.5 1.4 copy-start
  6.5 5.2 %copy-start.3 = (s32[8]{0:T(128)S(1)}, s32[8]{0:T(128)}, u32[]{:S(2)}) copy-start(s32[8]{0:T(128)} %param.15) | copy-start | bytes 100
  6.5 8.5 %copy-start.1 = (bf16[150,768]{1,0:T(8,128)(2,1)S(1)}, bf16[150,768]{1,0:T(8,128)(2,1)}, u32[]{:S(2)}) copy-start(bf16[150,768]{1,0:T(8,128)(2,1)} %param.8) | copy-start | bytes 691204
  6.5 9.2 %copy-start.2 = (bf16[150,768]{1,0:T(8,128)(2,1)S(1)}, bf16[150,768]{1,0:T(8,128)(2,1)}, u32[]{:S(2)}) copy-start(bf16[150,768]{1,0:T(8,128)(2,1)} %param.9) | copy-start | bytes 691204
  6.5 232.7 %all-gather.6.cloned.1.call-start = ((), (), s32[]{:S(2)}) async-start(), calls=%async_computation.3 | async-start | bytes 14155776 | tf_op jit(solution)/shard_map/all_gather | solution.py:17
  11.0 325.6 %all-gather.4.cloned.1.call-start = ((), (), s32[]{:S(2)}) async-start(), calls=%async_computation.1 | async-start | bytes 5308416 | tf_op jit(solution)/shard_map/all_gather | solution.py:151
  11.7 341.0 %reduce-scatter.2.cloned.1.call-start = ((), (), s32[]{:S(2)}) async-start(), calls=%async_computation.2 | async-start | bytes 1400832 | tf_op jit(solution)/shard_map/reduce_scatter | solution.py:154
  24.9 228.4 %collective-permute-start = (bf16[150,1536]{1,0:T(8,128)(2,1)}, bf16[150,1536]{1,0:T(8,128)(2,1)}, u32[]{:S(2)}, u32[]{:S(2)}) collective-permute-start(bf16[150,1536]{1,0:T(8,128)(2,1)} %pad_maximum_fusion.1), channel_id=1, source_target_pairs={{0,6},{2,8},{4,10},{6,12},{8,14},{10,0},{12,2},{14,4},{1,7},{3,9},... | collective-permute-start | bytes 1382408 | tf_op jit(solution)/shard_map/ppermute | solution.py:27
  28.9 227.2 %collective-permute-start.1 = (bf16[150,1536]{1,0:T(8,128)(2,1)}, bf16[150,1536]{1,0:T(8,128)(2,1)}, u32[]{:S(2)}, u32[]{:S(2)}) collective-permute-start(bf16[150,1536]{1,0:T(8,128)(2,1)} %pad_maximum_fusion.1), channel_id=1, source_target_pairs={{0,4},{2,6},{4,8},{6,10},{8,12},{10,14},{12,0},{14,2},{1,5},{3,7},... | collective-permute-start | bytes 1382408 | tf_op jit(solution)/shard_map/ppermute | solution.py:27
  30.5 225.6 %collective-permute-start.2 = (bf16[150,1536]{1,0:T(8,128)(2,1)}, bf16[150,1536]{1,0:T(8,128)(2,1)}, u32[]{:S(2)}, u32[]{:S(2)}) collective-permute-start(bf16[150,1536]{1,0:T(8,128)(2,1)} %pad_maximum_fusion.1), channel_id=1, source_target_pairs={{0,2},{2,4},{4,6},{6,8},{8,10},{10,12},{12,14},{14,0},{1,3},{3,5},... | collective-permute-start | bytes 1382408 | tf_op jit(solution)/shard_map/ppermute | solution.py:27
  32.1 224.0 %collective-permute-start.3 = (bf16[150,1536]{1,0:T(8,128)(2,1)}, bf16[150,1536]{1,0:T(8,128)(2,1)}, u32[]{:S(2)}, u32[]{:S(2)}) collective-permute-start(bf16[150,1536]{1,0:T(8,128)(2,1)} %pad_maximum_fusion.1), channel_id=1, source_target_pairs={{0,14},{2,0},{4,2},{6,4},{8,6},{10,8},{12,10},{14,12},{1,15},{3,1}... | collective-permute-start | bytes 1382408 | tf_op jit(solution)/shard_map/ppermute | solution.py:27
  35.2 220.9 %collective-permute-start.4 = (bf16[150,1536]{1,0:T(8,128)(2,1)}, bf16[150,1536]{1,0:T(8,128)(2,1)}, u32[]{:S(2)}, u32[]{:S(2)}) collective-permute-start(bf16[150,1536]{1,0:T(8,128)(2,1)} %pad_maximum_fusion.1), channel_id=1, source_target_pairs={{0,12},{2,14},{4,0},{6,2},{8,4},{10,6},{12,8},{14,10},{1,13},{3,15... | collective-permute-start | bytes 1382408 | tf_op jit(solution)/shard_map/ppermute | solution.py:27
  253.3 25.8 %collective-permute-start.5 = (bf16[150,1536]{1,0:T(8,128)(2,1)}, bf16[150,1536]{1,0:T(8,128)(2,1)}, u32[]{:S(2)}, u32[]{:S(2)}) collective-permute-start(bf16[150,1536]{1,0:T(8,128)(2,1)} %pad_maximum_fusion.1), channel_id=1, source_target_pairs={{0,10},{2,12},{4,14},{6,0},{8,2},{10,4},{12,6},{14,8},{1,11},{3,13... | collective-permute-start | bytes 1382408 | tf_op jit(solution)/shard_map/ppermute | solution.py:27
  315.3 11.4 %slice-start = ((s8[4939776]{0:T(1024)(128)(4,1)}), s8[4194304]{0:T(1024)(128)(4,1)S(1)}, s32[]{:S(2)}) async-start(s8[4939776]{0:T(1024)(128)(4,1)} %bitcast.17), calls=%async_computation.4 | async-start | bytes 8388608
  320.7 6.0 %slice-start.1 = ((s8[4939776]{0:T(1024)(128)(4,1)}), s8[745472]{0:T(1024)(128)(4,1)S(1)}, s32[]{:S(2)}) async-start(s8[4939776]{0:T(1024)(128)(4,1)} %bitcast.17), calls=%async_computation.5 | async-start | bytes 1490944
Sparse Core Ops, SparseCore 0:
  11.1 228.1 all-gather.5
  241.3 95.2 all-gather.3
  340.9 11.7 reduce-scatter.1
